TPU v7x, 32 devices: a whole 2x2x4 slice. The times are simulated.
32 devices in a mesh: chan: 4 (over x, core), tm: 8 (over z, y).
Axes of the slice: x: 2, y: 2, z: 4, core: 2. Of those that a mesh axis runs over, the one named last changes fastest.
Arguments:
- record: float32 [2048, 65536], P('chan', 'tm'), may hold values from -6 to 6
- whitening: float32 [65], replicated, may hold values from -0.75 to 0.75
- offsets: int32 [128], P('tm'), may hold values from 0 to 256, as said below
- window_valid: int32 [128], P('tm'), may hold values 0 or 1
Outputs:
- cross_spectra: bfloat16 [64, 2, 2048, 2048], P('tm', None, 'chan')
Inputs may be any that keep to these rules, and one draw needn't show every extreme that they name: `offsets`: some window has offset exactly 256.
All inputs are finite; a program needn't handle non-finite values. No bound on the sum of `window_valid` on one device may be relied on, other than what follows from the above.
Results may differ from a plain program's by a relative error of at most 0.006.
Values may be sent and summed in bfloat16 or wider, within the bound.
No kernel may reach another device: no remote copies, remote signals or barrier semaphores. Data moves between devices by JAX's collectives and lax.ppermute only.
A program may use at most 192 MiB of HBM per device.

v0:
```python
import functools
import math

import jax
import jax.numpy as jnp
import numpy as np
from jax import lax
from jax.experimental import pallas as pl
from jax.experimental.pallas import tpu as pltpu
from jax.sharding import PartitionSpec as P

L = 2048
HOP = 512
JITTER = 256
TAPS = 65
BINS = 64
K0 = 64
RIM = 128
GROUP = L // HOP
EDGE = RIM + JITTER
LANES = 2 * BINS
MIB = 1 << 20
F32 = jnp.float32
BF16 = jnp.bfloat16


def from_behind(shard, axis, by):
    devices = lax.axis_size(axis)
    pairs = [(i, i + by) for i in range(devices) if 0 <= i + by < devices]
    return lax.ppermute(shard, axis, pairs)


def phase_table():
    sample = np.arange(L) - (TAPS - 1)
    angles = 2.0 * np.pi * np.mod(sample[:, None] * (K0 + np.arange(BINS))[None, :], L) / L
    return (np.concatenate([np.cos(angles), -np.sin(angles)], axis=1) / math.sqrt(L)).astype(np.float32)


def matmul(a, b):
    return jnp.dot(a, b, preferred_element_type=F32)


def turn(values, place):
    lane = lax.broadcasted_iota(jnp.int32, (8, LANES), 1)
    bins = K0 + (lane & (BINS - 1))
    angles = ((bins * (place + L)) & (L - 1)).astype(F32) * (2.0 * math.pi / L)
    sine = jnp.sin(angles)
    sine = jnp.where(lane < BINS, -sine, sine)
    return values * jnp.cos(angles)[:1] + pltpu.roll(values, BINS, 1) * sine[:1]


def edge_table(rise, fall, offset):
    start = JITTER - offset
    return jnp.concatenate([rise[pl.ds(start, RIM), :], fall[pl.ds(start, JITTER), :]], axis=0).astype(BF16)


def across(values):
    channels = values.shape[0]
    if channels % 128:
        values = jnp.pad(values, ((0, 128 - channels), (0, 0)))
    return values.T


def outbox_kernel(offsets, valid, record, out):
    top = record[0:8, :]
    row = lax.broadcasted_iota(jnp.int32, top.shape, 0)
    lane = lax.broadcasted_iota(jnp.int32, top.shape, 1)
    first = offsets.shape[0] - GROUP
    for q in range(GROUP):
        top = jnp.where((row == 0) & (lane == q), offsets[first + q].astype(F32), top)
        top = jnp.where((row == 0) & (lane == GROUP + q), valid[first + q].astype(F32), top)
    out[...] = jnp.concatenate([top, record[8:, :]], axis=0).astype(BF16)


def outbox(record, offsets, valid):
    channels, slab = record.shape
    smem = pl.BlockSpec(memory_space=pltpu.SMEM)
    return pl.pallas_call(
        outbox_kernel,
        grid=(1,),
        out_shape=jax.ShapeDtypeStruct((channels, RIM), BF16),
        in_specs=[smem, smem, pl.BlockSpec((channels, RIM), lambda i: (0, slab // RIM - 1))],
        out_specs=pl.BlockSpec(memory_space=pltpu.VMEM),
        compiler_params=pltpu.CompilerParams(vmem_limit_bytes=60 * MIB),
        name="outbox",
    )(offsets, valid, record)


def tables_kernel(taps, table, blocks, rise, fall, padded):
    padded[0 : TAPS - 1, :] = jnp.zeros((TAPS - 1, LANES), F32)
    padded[TAPS - 1 :, :] = table[TAPS - 1 : TAPS - 1 + padded.shape[0] - (TAPS - 1), :]
    ramp = jnp.zeros((TAPS - 1, LANES), F32)
    gain = jnp.zeros((1, LANES), F32)
    for m in range(TAPS):
        tap = taps[m]
        ramp = ramp + tap * padded[m : m + TAPS - 1, :]
        gain = gain + tap * padded[TAPS - 1 + m : TAPS + m, :]
    gain = jnp.broadcast_to(gain * math.sqrt(L), (8, LANES))
    lane = lax.broadcasted_iota(jnp.int32, (8, LANES), 1)
    swapped = pltpu.roll(gain, BINS, 1)
    gain_re = jnp.where(lane < BINS, gain, swapped)[:1]
    gain_im = jnp.where(lane < BINS, -swapped, gain)[:1]
    columns = table[...]
    pure = columns * gain_re + pltpu.roll(columns, BINS, 1) * gain_im
    blocks[...] = pure.astype(BF16)
    rise[...] = jnp.zeros_like(rise)
    rise[rise.shape[0] - (TAPS - 1) :, :] = -ramp
    ahead = JITTER - (TAPS - 1)
    fall[0:ahead, :] = pure[L - ahead :]
    fall[ahead:JITTER, :] = pure[: TAPS - 1] - ramp
    fall[JITTER:, :] = jnp.zeros((fall.shape[0] - JITTER, LANES), F32)


def tables(whitening):
    vmem = pl.BlockSpec(memory_space=pltpu.VMEM)
    return pl.pallas_call(
        tables_kernel,
        out_shape=(
            jax.ShapeDtypeStruct((L, LANES), BF16),
            jax.ShapeDtypeStruct((EDGE, LANES), F32),
            jax.ShapeDtypeStruct((2 * JITTER, LANES), F32),
        ),
        in_specs=[pl.BlockSpec(memory_space=pltpu.SMEM), vmem],
        out_specs=(vmem, vmem, vmem),
        scratch_shapes=[pltpu.VMEM((2 * TAPS + 6, LANES), F32)],
        compiler_params=pltpu.CompilerParams(vmem_limit_bytes=16 * MIB),
        name="tables",
    )(whitening, phase_table())


def border_kernel(inbox, record, blocks, rise, fall, parts, done, collected):
    channels = record.shape[0]
    done[...] = jnp.zeros_like(done)
    head = inbox[0:16, :].astype(F32)[:1]
    lane = lax.broadcasted_iota(jnp.int32, (1, LANES), 1)

    def told(at):
        return jnp.sum(jnp.where(lane == at, head, 0.0)).astype(jnp.int32)

    before = jnp.zeros((channels, LANES), F32)
    for q in range(GROUP):
        offset = told(q)
        edges = edge_table(rise, fall, offset)
        if q == 0:
            part = matmul(record[:, 0:JITTER].astype(BF16), edges[RIM:])
        else:
            part = matmul(record[:, HOP * q - RIM : HOP * q + JITTER].astype(BF16), edges)
        place = HOP * q + offset - (TAPS - 1)
        part = (part + turn(before, place)) * told(GROUP + q).astype(F32)
        upright = across(part)
        for c in range(collected.shape[0]):
            piece = upright[:, 128 * c : 128 * c + 128]
            collected[c, pl.ds(q, BINS, stride=2 * GROUP), :] = piece[:BINS]
            collected[c, pl.ds(GROUP + q, BINS, stride=2 * GROUP), :] = piece[BINS:]
        if q < GROUP - 1:
            before = before + matmul(
                record[:, HOP * q : HOP * q + HOP].astype(BF16), blocks[HOP * q : HOP * q + HOP, :]
            )
    width = min(128, channels)
    for c in range(collected.shape[0]):
        block = collected[c].reshape(BINS, 2 * GROUP, 128).astype(BF16)
        parts[:, :, width * c : width * c + width] = block[:, :, :width]


def border_parts(record, inbox, blocks, rise, fall):
    channels = record.shape[0]
    vmem = pl.BlockSpec(memory_space=pltpu.VMEM)
    lead = L - HOP + JITTER
    return pl.pallas_call(
        border_kernel,
        grid=(1,),
        out_shape=(jax.ShapeDtypeStruct((BINS, 2 * GROUP, channels), BF16), jax.ShapeDtypeStruct((8, 128), F32)),
        in_specs=[vmem, pl.BlockSpec((channels, lead), lambda i: (0, 0)), vmem, vmem, vmem],
        out_specs=(vmem, vmem),
        scratch_shapes=[pltpu.VMEM((max(channels // 128, 1), 2 * GROUP * BINS, 128), F32)],
        compiler_params=pltpu.CompilerParams(vmem_limit_bytes=50 * MIB),
        cost_estimate=pl.CostEstimate(
            flops=2 * channels * LANES * 3072, bytes_accessed=4 * channels * lead, transcendentals=0
        ),
        name="border_parts",
    )(inbox, record, blocks, rise, fall)


def spectra_kernel(first, span, offsets, valid, record, rim, blocks, rise, fall, parts, *rest):
    *outs, done, samples, later, collected, sems = rest
    channels, slab = record.shape
    windows = GROUP * span
    tail = L - HOP + JITTER
    done[...] = jnp.zeros_like(done)
    end = RIM + L * span
    base = L * first
    fetches = [(base + HOP * i, RIM + HOP * i, HOP) for i in range(GROUP * span)]
    if first == 0:
        samples[:, 0:RIM] = rim[...].astype(F32)
    else:
        fetches[0] = (base - RIM, 0, RIM + HOP)
    more = base + L * span < slab
    if more:
        fetches += [(base + HOP * i, RIM + HOP * i, HOP) for i in range(GROUP * span, GROUP * (span + 1) - 1)]
        left = tail - HOP * (GROUP - 1)
        fetches.append((base + L * span + tail - left, end + tail - left, left))
    else:
        samples[:, end:] = jnp.zeros((channels, tail), F32)
    copies = [
        pltpu.make_async_copy(record.at[:, pl.ds(src, size)], samples.at[:, pl.ds(dst, size)], sems.at[i])
        for i, (src, dst, size) in enumerate(fetches)
    ]
    for copy in copies:
        copy.start()

    def arrived(i):
        if i < len(copies):
            copies[i].wait()

    def block_sums(s):
        found = []
        for i in range(GROUP if s < span else GROUP - 1):
            arrived(GROUP * s + i)
            found.append(
                matmul(
                    samples[:, RIM + L * s + HOP * i : RIM + L * s + HOP * i + HOP].astype(BF16),
                    blocks[HOP * i : HOP * i + HOP, :],
                )
            )
        return found

    def keep(found):
        total = found[GROUP - 1]
        later[GROUP - 1] = total
        for q in range(GROUP - 2, -1, -1):
            total = total + found[q]
            later[q] = total

    keep(block_sums(0))
    for s in range(span):
        found = block_sums(s + 1) if s + 1 < span or more else []
        if s + 1 == span and more:
            arrived(len(copies) - 1)
        before = None
        for q in range(GROUP):
            w = GROUP * s + q
            offset = offsets[GROUP * first + w]
            begin = HOP * w
            ends = samples[:, begin + L : begin + L + EDGE] - samples[:, begin : begin + EDGE]
            part = matmul(ends.astype(BF16), edge_table(rise, fall, offset))
            total = later[q] if before is None else later[q] + before
            part = (part + turn(total, HOP * q + offset - (TAPS - 1))) * valid[GROUP * first + w].astype(F32)
            upright = across(part)
            for c in range(collected.shape[0]):
                piece = upright[:, 128 * c : 128 * c + 128]
                collected[c, pl.ds(w, BINS, stride=2 * windows), :] = piece[:BINS]
                collected[c, pl.ds(windows + w, BINS, stride=2 * windows), :] = piece[BINS:]
            if found and q < GROUP - 1:
                before = found[q] if before is None else before + found[q]
        if s + 1 < span:
            keep(found)

    width = min(128, channels)
    for c in range(collected.shape[0]):
        lanes = slice(width * c, width * c + width)
        block = collected[c].reshape(BINS, 2 * windows, 128)[:, :, :width]
        if not more:
            block = with_parts(block, parts[:, :, lanes].astype(F32))
        block = block.astype(BF16)
        for group in range(outs[0].shape[0]):
            begin = group * BINS // outs[0].shape[0]
            for out in outs:
                out[group, :, :, lanes] = block[begin : begin + out.shape[1]]
                begin += out.shape[1]


def with_parts(block, part):
    windows = block.shape[1] // 2
    row = lax.broadcasted_iota(jnp.int32, part.shape, 1)
    moved = jnp.concatenate([part[:, GROUP:], part[:, :GROUP]], axis=1)
    pieces = []
    for ri, extra in enumerate((moved, part)):
        end = windows * ri + windows
        if windows > 2 * GROUP:
            pieces.append(block[:, windows * ri : end - 2 * GROUP])
        pieces.append(block[:, end - 2 * GROUP : end] + jnp.where(row >= GROUP, extra, 0.0))
    return jnp.concatenate(pieces, axis=1)


def chunk_sizes(bins):
    return [bins - 3 * bins // 8, 3 * bins // 8]


def own_spectra(record, rim, offsets, valid, transform, rise, fall, parts, devices, half):
    channels, slab = record.shape
    span = slab // L // 2
    windows = GROUP * span
    sizes = chunk_sizes(BINS // devices) if half else [BINS // devices]
    smem = pl.BlockSpec(memory_space=pltpu.SMEM)
    vmem = pl.BlockSpec(memory_space=pltpu.VMEM)
    *chunks, done = pl.pallas_call(
        functools.partial(spectra_kernel, span * half, span),
        out_shape=tuple(jax.ShapeDtypeStruct((devices, count, 2 * windows, channels), BF16) for count in sizes)
        + (jax.ShapeDtypeStruct((8, 128), F32),),
        in_specs=[smem, smem, pl.BlockSpec(memory_space=pl.ANY), vmem, vmem, vmem, vmem, vmem],
        out_specs=(vmem,) * (len(sizes) + 1),
        scratch_shapes=[
            pltpu.VMEM((channels, RIM + L * span + L - HOP + JITTER), F32),
            pltpu.VMEM((GROUP, channels, LANES), F32),
            pltpu.VMEM((max(channels // 128, 1), LANES * windows, 128), F32),
            pltpu.SemaphoreType.DMA((GROUP * (span + 1),)),
        ],
        compiler_params=pltpu.CompilerParams(vmem_limit_bytes=50 * MIB),
        cost_estimate=pl.CostEstimate(
            flops=2 * channels * LANES * 896 * windows, bytes_accessed=2 * channels * slab, transcendentals=0
        ),
        name=f"own_spectra_{half}",
    )(offsets, valid, record, rim, transform, rise, fall, parts)
    return chunks, done


def left_kernel(early, late, done, out, ready):
    ready[...] = jnp.zeros_like(ready)
    sources, _, rows, channels = early.shape
    depth = sources * rows
    half = rows // 2
    for i, own in enumerate((early, late)):
        straight = own[:, 0].astype(F32)
        turned = jnp.concatenate([straight[:, half:], -straight[:, :half]], axis=1)
        for j, side in enumerate((straight, turned)):
            out[0, channels * j : channels * j + channels, depth * i : depth * i + depth] = (
                side.reshape(depth, channels).T.astype(BF16)
            )


def left_sides(early, late, begin, done):
    sources, count, rows, channels = late.shape
    shape = (count, 2 * channels, 2 * sources * rows)
    vmem = pl.BlockSpec(memory_space=pltpu.VMEM)
    return pl.pallas_call(
        left_kernel,
        grid=(count,),
        out_shape=(jax.ShapeDtypeStruct(shape, BF16), jax.ShapeDtypeStruct((8, 128), F32)),
        in_specs=[
            pl.BlockSpec((sources, 1, rows, channels), lambda f: (0, begin + f, 0, 0)),
            pl.BlockSpec((sources, 1, rows, channels), lambda f: (0, f, 0, 0)),
            vmem,
        ],
        out_specs=(pl.BlockSpec((1,) + shape[1:], lambda f: (f, 0, 0)), vmem),
        compiler_params=pltpu.CompilerParams(vmem_limit_bytes=16 * MIB),
        name="left_sides",
    )(early, late, done)


def cross_kernel(scale, side, me, left, *rest):
    out, done = rest[-2:]
    done[...] = jnp.zeros_like(done)
    sources, _, rows, channels = rest[0].shape[-4:]
    depth = sources * rows
    blocks = out.shape[3] // channels
    tile = min(256, channels)
    for n in range(blocks):
        if side is None:
            pair = [rest[0][n], rest[1][n]]
            at = channels * n
        else:
            pair = [rest[2 * n][...], rest[2 * n + 1][...]]
            at = pl.multiple_of(channels * ((me[0] ^ n) & (blocks - 1)), 128)
        right = jnp.concatenate([one[:, 0].reshape(depth, channels) for one in pair], axis=0)
        for j in range(0, channels, tile):
            for r in range(0, 2 * channels, tile):
                both = matmul(left[0, r : r + tile, :], right[:, j : j + tile]) * scale
                out[0, r // channels, r % channels : r % channels + tile, pl.ds(at + j, tile)] = both.astype(BF16)


def cross_products(left, early, late, result, begin, bins, blocks, side):
    sources, count, rows, channels = (late if side is None else late[0]).shape[-4:]
    columns = blocks if side is None else len(late)
    shape = (bins, 2, channels, blocks * channels)
    operands = [lax.axis_index("chan").astype(jnp.int32).reshape(1), left]
    in_specs = [pl.BlockSpec((1,) + left.shape[1:], lambda f, me: (f, 0, 0))]
    if side is None:
        operands += [early, late]
        in_specs += [
            pl.BlockSpec((blocks, sources, 1, rows, channels), lambda f, me: (0, 0, begin + f, 0, 0)),
            pl.BlockSpec((blocks, sources, 1, rows, channels), lambda f, me: (0, 0, f, 0, 0)),
        ]
    else:
        for pair in zip(early, late):
            operands += pair
            in_specs += [
                pl.BlockSpec((sources, 1, rows, channels), lambda f, me: (0, begin + f, 0, 0)),
                pl.BlockSpec((sources, 1, rows, channels), lambda f, me: (0, f, 0, 0)),
            ]
    if result is None:
        result, aliases = operands[1], {}
    else:
        aliases = {len(operands): 0}
    operands.append(result)
    in_specs.append(pl.BlockSpec(memory_space=pl.ANY))
    depth = 2 * sources * rows

    def place(f, me):
        return begin + f, 0, 0, 0 if side is None else (me[0] // columns) ^ side

    return pl.pallas_call(
        functools.partial(cross_kernel, 2.0 / depth, side),
        grid_spec=pltpu.PrefetchScalarGridSpec(
            num_scalar_prefetch=1,
            grid=(count,),
            in_specs=in_specs,
            out_specs=(
                pl.BlockSpec((1, 2, channels, columns * channels), place),
                pl.BlockSpec((8, 128), lambda f, me: (0, 0)),
            ),
        ),
        out_shape=(jax.ShapeDtypeStruct(shape, BF16), jax.ShapeDtypeStruct((8, 128), F32)),
        input_output_aliases=aliases,
        compiler_params=pltpu.CompilerParams(vmem_limit_bytes=24 * MIB),
        cost_estimate=pl.CostEstimate(
            flops=4 * count * channels * columns * channels * depth,
            bytes_accessed=4 * count * channels * columns * channels,
            transcendentals=0,
        ),
        name="cross_products",
    )(*operands)


def swapped(shard, axis, bit):
    devices = lax.axis_size(axis)
    return lax.ppermute(shard, axis, [(i, i ^ bit) for i in range(devices)])


def fan(shard, axis, bit):
    held = {0: shard}
    while bit:
        held.update({n | bit: swapped(block, axis, bit) for n, block in list(held.items())})
        bit //= 2
    return held


def after_kernel(shard, done, out):
    out[...] = shard[...]


def after(shard, done):
    if done is None:
        return shard
    vmem = pl.BlockSpec(memory_space=pltpu.VMEM)
    return pl.pallas_call(
        after_kernel,
        out_shape=jax.ShapeDtypeStruct(shard.shape, shard.dtype),
        in_specs=[vmem, vmem],
        out_specs=vmem,
        compiler_params=pltpu.CompilerParams(vmem_limit_bytes=8 * MIB),
        name="after",
    )(shard, done)


def per_device(record, whitening, offsets, window_valid):
    devices = lax.axis_size("tm")
    blocks = lax.axis_size("chan")
    stacked = blocks & (blocks - 1) != 0 or record.shape[0] % 128 != 0
    top = blocks // 2
    bins = BINS // devices

    def exchanged(chunk):
        return lax.all_to_all(chunk, "tm", split_axis=0, concat_axis=0, tiled=True)

    def fanned(shard):
        held = fan(shard, "chan", top // 2)
        return [held[n] for n in range(top)]

    inbox = from_behind(outbox(record, offsets, window_valid), "tm", 1)
    transform, rise, fall = tables(whitening)
    parts, done = border_parts(record, inbox, transform, rise, fall)
    parts = from_behind(parts, "tm", -1)
    views = record, inbox, offsets, window_valid, transform, rise, fall
    (early,), _ = own_spectra(*views, done, devices, 0)
    late, done = own_spectra(*views, parts, devices, 1)
    early = after(exchanged(after(early, parts)), done)
    result, begin, rest = None, 0, []
    near_early = None if stacked else fanned(early)
    far_early = None if stacked else swapped(early, "chan", top)
    for p, chunk in enumerate(late):
        mine = exchanged(chunk)
        if stacked:
            left, _ = left_sides(early, mine, begin, done)
            both = [lax.all_gather(one, "chan", axis=0, tiled=False) for one in (early, mine)]
            result, _ = cross_products(left, *both, result, begin, bins, blocks, None)
        else:
            mine = after(mine, done) if p else mine
            far, near = swapped(mine, "chan", top), fanned(mine)
            left, _ = left_sides(early, mine, begin, done)
            result, done = cross_products(left, near_early, near, result, begin, bins, blocks, 0)
            rest.append((left, far, begin))
        begin += mine.shape[1]
    if not stacked:
        far_early, ready = fanned(after(far_early, mine)), None
        for left, far, begin in rest:
            far = fanned(after(far, ready))
            result, ready = cross_products(left, far_early, far, result, begin, bins, blocks, 1)
    return result


def solution(mesh):
    in_specs = (P("chan", "tm"), P(), P("tm"), P("tm"))
    out_specs = P("tm", None, "chan", None)
    return jax.shard_map(
        per_device, mesh=mesh, in_specs=in_specs, out_specs=out_specs, check_vma=False
    )
```

profile of v0, /device:TPU:0, one launch (start us, length us, event | category | flops | bytes accessed | tf_op | source)
XLA Modules:
  0.0 123.3 jit_solution(3069510751326076394)
XLA Ops:
  0.0 1.7 %outbox.1 = bf16[512,128]{1,0:T(8,128)(2,1)} custom-call(s32[16]{0:T(128)} %offsets.5, s32[16]{0:T(128)} %valid.5, f32[512,8192]{1,0:T(8,128)} %record.7), custom_call_target="tpu_custom_call" | custom-call | tf_op jit(solution)/shard_map/outbox/pallas_call | solution.py:78
  1.7 4.9 %collective-permute-start = (bf16[512,128]{1,0:T(8,128)(2,1)}, bf16[512,128]{1,0:T(8,128)(2,1)S(1)}, u32[]{:S(2)}, u32[]{:S(2)}) collective-permute-start(bf16[512,128]{1,0:T(8,128)(2,1)} %outbox.1), channel_id=1, source_target_pairs={{0,1},{1,2},{2,3},{3,4},{4,5},{5,6},{6,7},{8,9},{9,10},{10,11},{11... | collective-permute-start | bytes 393224 | tf_op jit(solution)/shard_map/ppermute | solution.py:30
  9.6 3.3 %border_parts.1 = (bf16[64,8,512]{2,1,0:T(8,128)(2,1)S(1)}, f32[8,128]{1,0:T(8,128)S(1)}) custom-call(bf16[512,128]{1,0:T(8,128)(2,1)S(1)} %collective-permute-done.inbox.rim, f32[512,8192]{1,0:T(8,128)} %record.7, bf16[2048,128]{1,0:T(8,128)(2,1)S(1)} %get-tuple-element.22.blocks, f32[384,128]{1,0:T(8,128)S(1)} %get-tuple-element.23.rise, ...), custom_call_target="tpu_custom_call" | custom-call | flops 402653184 | bytes 3670016 | tf_op jit(solution)/shard_map/border_parts/pallas_call | solution.py:169
  12.9 1.3 %collective-permute-start.1 = (bf16[64,8,512]{2,1,0:T(8,128)(2,1)S(1)}, bf16[64,8,512]{2,1,0:T(8,128)(2,1)S(1)}, u32[]{:S(2)}, u32[]{:S(2)}) collective-permute-start(bf16[64,8,512]{2,1,0:T(8,128)(2,1)S(1)} %get-tuple-element.27), channel_id=1, source_target_pairs={{1,0},{2,1},{3,2},{4,3},{5,4},{6,5},{7,6},{9,8},{10,9},{11,10},{12... | collective-permute-start | bytes 1572872 | tf_op jit(solution)/shard_map/ppermute | solution.py:30
  14.2 8.1 %own_spectra_0.1 = (bf16[8,8,16,512]{3,2,1,0:T(8,128)(2,1)S(1)}, f32[8,128]{1,0:T(8,128)}) custom-call(s32[16]{0:T(128)S(1)} %copy-done.3, s32[16]{0:T(128)S(1)} %copy-done.4, f32[512,8192]{1,0:T(8,128)} %record.7, bf16[512,128]{1,0:T(8,128)(2,1)S(1)} %collective-permute-done.inbox.rim, bf16[2048,128]{1,0:T(8,128)(2,1)S(1)} %get-tuple-element.22.blocks, ...), custom_call_target="tpu_custom_call" | custom-call | flops 939524096 | bytes 8388608 | tf_op jit(solution)/shard_map/own_spectra_0/pallas_call | solution.py:296
  22.3 6.0 %collective-permute-done.1.done.parts = bf16[64,8,512]{2,1,0:T(8,128)(2,1)S(1)} collective-permute-done((bf16[64,8,512]{2,1,0:T(8,128)(2,1)S(1)}, bf16[64,8,512]{2,1,0:T(8,128)(2,1)S(1)}, u32[]{:S(2)}, u32[]{:S(2)}) %collective-permute-start.1) | collective-permute-done | bytes 524320 | tf_op jit(solution)/shard_map/ppermute | solution.py:30
  29.3 6.0 %all-to-all-start = ((bf16[8,8,16,512]{3,2,1,0:T(8,128)(2,1)}), bf16[8,8,16,512]{3,2,1,0:T(8,128)(2,1)S(1)}, u32[]{:S(2)}, u32[]{:S(2)}) async-start(bf16[8,8,16,512]{3,2,1,0:T(8,128)(2,1)} %after.5), calls=%async_computation | async-start | bytes 2097152 | tf_op jit(solution)/shard_map/all_to_all | solution.py:463
  35.3 8.3 %own_spectra_1.1 = (bf16[8,5,16,512]{3,2,1,0:T(8,128)(2,1)}, bf16[8,3,16,512]{3,2,1,0:T(8,128)(2,1)}, f32[8,128]{1,0:T(8,128)S(1)}) custom-call(s32[16]{0:T(128)S(1)} %copy-done.3, s32[16]{0:T(128)S(1)} %copy-done.4, f32[512,8192]{1,0:T(8,128)} %record.7, bf16[512,128]{1,0:T(8,128)(2,1)S(1)} %collective-permute-done.inbox.rim, ...), custom_call_target="tpu_custom_call" | custom-call | flops 939524096 | bytes 8388608 | tf_op jit(solution)/shard_map/own_spectra_1/pallas_call | solution.py:296
  43.6 15.8 %all-to-all-done.shard = bf16[8,8,16,512]{3,2,1,0:T(8,128)(2,1)S(1)} async-done(((bf16[8,8,16,512]{3,2,1,0:T(8,128)(2,1)}), bf16[8,8,16,512]{3,2,1,0:T(8,128)(2,1)S(1)}, u32[]{:S(2)}, u32[]{:S(2)}) %all-to-all-start) | async-done | bytes 1048608 | tf_op jit(solution)/shard_map/all_to_all | solution.py:463
  59.5 3.5 %all-to-all-start.2 = ((bf16[8,5,16,512]{3,2,1,0:T(8,128)(2,1)}), bf16[8,5,16,512]{3,2,1,0:T(8,128)(2,1)S(1)}, u32[]{:S(2)}, u32[]{:S(2)}) async-start(bf16[8,5,16,512]{3,2,1,0:T(8,128)(2,1)} %get-tuple-element.30), calls=%async_computation.2 | async-start | bytes 1310720 | tf_op jit(solution)/shard_map/all_to_all | solution.py:463
  63.2 1.6 %collective-permute-start.4 = (bf16[8,8,16,512]{3,2,1,0:T(8,128)(2,1)S(1)}, bf16[8,8,16,512]{3,2,1,0:T(8,128)(2,1)}, u32[]{:S(2)}, u32[]{:S(2)}) collective-permute-start(bf16[8,8,16,512]{3,2,1,0:T(8,128)(2,1)S(1)} %after.6.early.rest_0_), channel_id=1, source_target_pairs={{0,16},{8,24},{16,0},{24,8},{1,17},{9,25},{17,1},{25,9},{2,18},{10... | collective-permute-start | bytes 3145736 | tf_op jit(solution)/shard_map/ppermute | solution.py:426
  64.7 15.3 %all-to-all-done.2.late.rest_1_ = bf16[8,5,16,512]{3,2,1,0:T(8,128)(2,1)S(1)} async-done(((bf16[8,5,16,512]{3,2,1,0:T(8,128)(2,1)}), bf16[8,5,16,512]{3,2,1,0:T(8,128)(2,1)S(1)}, u32[]{:S(2)}, u32[]{:S(2)}) %all-to-all-start.2) | async-done | bytes 655392 | tf_op jit(solution)/shard_map/all_to_all | solution.py:463
  80.0 3.7 %all-to-all-start.1 = ((bf16[8,3,16,512]{3,2,1,0:T(8,128)(2,1)}), bf16[8,3,16,512]{3,2,1,0:T(8,128)(2,1)S(1)}, u32[]{:S(2)}, u32[]{:S(2)}) async-start(bf16[8,3,16,512]{3,2,1,0:T(8,128)(2,1)} %get-tuple-element.29), calls=%async_computation.1 | async-start | bytes 786432 | tf_op jit(solution)/shard_map/all_to_all | solution.py:463
  83.7 1.6 %collective-permute-start.6 = (bf16[8,5,16,512]{3,2,1,0:T(8,128)(2,1)S(1)}, bf16[8,5,16,512]{3,2,1,0:T(8,128)(2,1)S(1)}, u32[]{:S(2)}, u32[]{:S(2)}) collective-permute-start(bf16[8,5,16,512]{3,2,1,0:T(8,128)(2,1)S(1)} %all-to-all-done.2.late.rest_1_), channel_id=1, source_target_pairs={{0,16},{8,24},{16,0},{24,8},{1,17},{9,25},{17,1},{25,9},{2,18},{10... | collective-permute-start | bytes 1966088 | tf_op jit(solution)/shard_map/ppermute | solution.py:426
  85.2 1.7 %left_sides.2 = (bf16[5,1024,256]{2,1,0:T(8,128)(2,1)S(1)}, f32[8,128]{1,0:T(8,128)}) custom-call(bf16[8,8,16,512]{3,2,1,0:T(8,128)(2,1)S(1)} %after.6.early.rest_0_, bf16[8,5,16,512]{3,2,1,0:T(8,128)(2,1)S(1)} %all-to-all-done.2.late.rest_1_, f32[8,128]{1,0:T(8,128)S(1)} %get-tuple-element.28.done), custom_call_target="tpu_custom_call" | custom-call | tf_op jit(solution)/shard_map/left_sides/pallas_call | solution.py:335
  87.0 7.1 %cross_products.4 = (bf16[8,2,512,2048]{3,2,1,0:T(8,128)(2,1)}, f32[8,128]{1,0:T(8,128)S(1)}) custom-call(s32[1]{0:T(128)} %bitcast.me, bf16[5,1024,256]{2,1,0:T(8,128)(2,1)S(1)} %get-tuple-element.31.left.rest_4_, bf16[8,8,16,512]{3,2,1,0:T(8,128)(2,1)S(1)} %after.6.early.rest_0_, bf16[8,5,16,512]{3,2,1,0:T(8,128)(2,1)S(1)} %all-to-all-done.2.late.rest_1_, ...), custom_call_target="tpu_custom_call" | custom-call | flops 2684354560 | bytes 10485760 | tf_op jit(solution)/shard_map/cross_products/pallas_call | solution.py:401
  94.0 1.5 %copy-done = bf16[5,1024,256]{2,1,0:T(8,128)(2,1)} copy-done((bf16[5,1024,256]{2,1,0:T(8,128)(2,1)}, bf16[5,1024,256]{2,1,0:T(8,128)(2,1)S(1)}, u32[]{:S(2)}) %copy-start) | copy-done | bytes 2621464
  96.1 1.4 %after.8.rest_0_ = bf16[8,8,16,512]{3,2,1,0:T(8,128)(2,1)S(1)} custom-call(bf16[8,8,16,512]{3,2,1,0:T(8,128)(2,1)} %collective-permute-done.4.shard, bf16[8,3,16,512]{3,2,1,0:T(8,128)(2,1)S(1)} %after.7.late.done.rest_1_), custom_call_target="tpu_custom_call" | custom-call | tf_op jit(solution)/shard_map/after/pallas_call | solution.py:445
  97.6 5.2 %collective-permute-done.6.rest_1_ = bf16[8,5,16,512]{3,2,1,0:T(8,128)(2,1)S(1)} collective-permute-done((bf16[8,5,16,512]{3,2,1,0:T(8,128)(2,1)S(1)}, bf16[8,5,16,512]{3,2,1,0:T(8,128)(2,1)S(1)}, u32[]{:S(2)}, u32[]{:S(2)}) %collective-permute-start.6) | collective-permute-done | bytes 655392 | tf_op jit(solution)/shard_map/ppermute | solution.py:426
  104.5 1.5 %collective-permute-start.5 = (bf16[8,3,16,512]{3,2,1,0:T(8,128)(2,1)S(1)}, bf16[8,3,16,512]{3,2,1,0:T(8,128)(2,1)S(1)}, u32[]{:S(2)}, u32[]{:S(2)}) collective-permute-start(bf16[8,3,16,512]{3,2,1,0:T(8,128)(2,1)S(1)} %after.7.late.done.rest_1_), channel_id=1, source_target_pairs={{0,16},{8,24},{16,0},{24,8},{1,17},{9,25},{17,1},{25,9},{2,18},{10... | collective-permute-start | bytes 1179656 | tf_op jit(solution)/shard_map/ppermute | solution.py:426
  106.0 5.0 %cross_products.5 = (bf16[8,2,512,2048]{3,2,1,0:T(8,128)(2,1)}, f32[8,128]{1,0:T(8,128)}) custom-call(s32[1]{0:T(128)} %bitcast.me, bf16[3,1024,256]{2,1,0:T(8,128)(2,1)S(1)} %get-tuple-element.33.left, bf16[8,8,16,512]{3,2,1,0:T(8,128)(2,1)S(1)} %after.6.early.rest_0_, ...), custom_call_target="tpu_custom_call", output_to_operand_aliasing={{0}: (6, {})} | custom-call | flops 1610612736 | bytes 6291456 | tf_op jit(solution)/shard_map/cross_products/pallas_call | solution.py:401
  111.1 6.3 %cross_products.6 = (bf16[8,2,512,2048]{3,2,1,0:T(8,128)(2,1)}, f32[8,128]{1,0:T(8,128)S(1)}) custom-call(s32[1]{0:T(128)} %bitcast.me, bf16[5,1024,256]{2,1,0:T(8,128)(2,1)S(1)} %copy-done.1, bf16[8,8,16,512]{3,2,1,0:T(8,128)(2,1)S(1)} %after.8.rest_0_, bf16[8,5,16,512]{3,2,1,0:T(8,128)(2,1)S(1)} %collective-permute-done.6.rest_1_, ...), custom_call_target="tpu_custom_call", output_to_operand_aliasing={{0}: (6, {})} | custom-call | flops 2684354560 | bytes 10485760 | tf_op jit(solution)/shard_map/cross_products/pallas_call | solution.py:401
  117.4 1.7 %collective-permute-done.10.rest_3_ = bf16[8,3,16,512]{3,2,1,0:T(8,128)(2,1)S(1)} collective-permute-done((bf16[8,3,16,512]{3,2,1,0:T(8,128)(2,1)S(1)}, bf16[8,3,16,512]{3,2,1,0:T(8,128)(2,1)S(1)}, u32[]{:S(2)}, u32[]{:S(2)}) %collective-permute-start.10) | collective-permute-done | bytes 393248 | tf_op jit(solution)/shard_map/ppermute | solution.py:426
  119.1 4.2 %cross_products.7 = (bf16[8,2,512,2048]{3,2,1,0:T(8,128)(2,1)}, f32[8,128]{1,0:T(8,128)}) custom-call(s32[1]{0:T(128)} %bitcast.me, bf16[3,1024,256]{2,1,0:T(8,128)(2,1)S(1)} %get-tuple-element.33.left, bf16[8,8,16,512]{3,2,1,0:T(8,128)(2,1)S(1)} %after.8.rest_0_, bf16[8,3,16,512]{3,2,1,0:T(8,128)(2,1)S(1)} %after.9.rest_1_, ...), custom_call_target="tpu_custom_call", output_to_operand_aliasing={{0}: (6, {})} | custom-call | flops 1610612736 | bytes 6291456 | tf_op jit(solution)/shard_map/cross_products/pallas_call | solution.py:401
  (32 shorter events, 6.7 us)
Async XLA Ops:
  0.0 14.2 %copy-start.3 = (s32[16]{0:T(128)S(1)}, s32[16]{0:T(128)}, u32[]{:S(2)}) copy-start(s32[16]{0:T(128)} %offsets.5) | copy-start | bytes 196
  0.0 14.2 %copy-start.4 = (s32[16]{0:T(128)S(1)}, s32[16]{0:T(128)}, u32[]{:S(2)}) copy-start(s32[16]{0:T(128)} %valid.5) | copy-start | bytes 196
  1.7 7.9 %collective-permute-start = (bf16[512,128]{1,0:T(8,128)(2,1)}, bf16[512,128]{1,0:T(8,128)(2,1)S(1)}, u32[]{:S(2)}, u32[]{:S(2)}) collective-permute-start(bf16[512,128]{1,0:T(8,128)(2,1)} %outbox.1), channel_id=1, source_target_pairs={{0,1},{1,2},{2,3},{3,4},{4,5},{5,6},{6,7},{8,9},{9,10},{10,11},{11... | collective-permute-start | bytes 393224 | tf_op jit(solution)/shard_map/ppermute | solution.py:30
  6.5 1.2 copy-start.2
  7.8 0.7 copy-start.5
  12.9 15.3 %collective-permute-start.1 = (bf16[64,8,512]{2,1,0:T(8,128)(2,1)S(1)}, bf16[64,8,512]{2,1,0:T(8,128)(2,1)S(1)}, u32[]{:S(2)}, u32[]{:S(2)}) collective-permute-start(bf16[64,8,512]{2,1,0:T(8,128)(2,1)S(1)} %get-tuple-element.27), channel_id=1, source_target_pairs={{1,0},{2,1},{3,2},{4,3},{5,4},{6,5},{7,6},{9,8},{10,9},{11,10},{12... | collective-permute-start | bytes 1572872 | tf_op jit(solution)/shard_map/ppermute | solution.py:30
  29.3 30.2 %all-to-all-start = ((bf16[8,8,16,512]{3,2,1,0:T(8,128)(2,1)}), bf16[8,8,16,512]{3,2,1,0:T(8,128)(2,1)S(1)}, u32[]{:S(2)}, u32[]{:S(2)}) async-start(bf16[8,8,16,512]{3,2,1,0:T(8,128)(2,1)} %after.5), calls=%async_computation | async-start | bytes 2097152 | tf_op jit(solution)/shard_map/all_to_all | solution.py:463
  59.5 20.6 %all-to-all-start.2 = ((bf16[8,5,16,512]{3,2,1,0:T(8,128)(2,1)}), bf16[8,5,16,512]{3,2,1,0:T(8,128)(2,1)S(1)}, u32[]{:S(2)}, u32[]{:S(2)}) async-start(bf16[8,5,16,512]{3,2,1,0:T(8,128)(2,1)} %get-tuple-element.30), calls=%async_computation.2 | async-start | bytes 1310720 | tf_op jit(solution)/shard_map/all_to_all | solution.py:463
  63.1 23.9 %collective-permute-start.2 = (bf16[8,8,16,512]{3,2,1,0:T(8,128)(2,1)S(1)}, bf16[8,8,16,512]{3,2,1,0:T(8,128)(2,1)}, u32[]{:S(2)}, u32[]{:S(2)}) collective-permute-start(bf16[8,8,16,512]{3,2,1,0:T(8,128)(2,1)S(1)} %after.6.early.rest_0_), channel_id=1, source_target_pairs={{0,8},{8,0},{16,24},{24,16},{1,9},{9,1},{17,25},{25,17},{2,10},{10... | collective-permute-start | bytes 3145736 | tf_op jit(solution)/shard_map/ppermute | solution.py:426
  63.2 32.9 %collective-permute-start.4 = (bf16[8,8,16,512]{3,2,1,0:T(8,128)(2,1)S(1)}, bf16[8,8,16,512]{3,2,1,0:T(8,128)(2,1)}, u32[]{:S(2)}, u32[]{:S(2)}) collective-permute-start(bf16[8,8,16,512]{3,2,1,0:T(8,128)(2,1)S(1)} %after.6.early.rest_0_), channel_id=1, source_target_pairs={{0,16},{8,24},{16,0},{24,8},{1,17},{9,25},{17,1},{25,9},{2,18},{10... | collective-permute-start | bytes 3145736 | tf_op jit(solution)/shard_map/ppermute | solution.py:426
  80.0 6.9 %collective-permute-start.3 = (bf16[8,5,16,512]{3,2,1,0:T(8,128)(2,1)S(1)}, bf16[8,5,16,512]{3,2,1,0:T(8,128)(2,1)S(1)}, u32[]{:S(2)}, u32[]{:S(2)}) collective-permute-start(bf16[8,5,16,512]{3,2,1,0:T(8,128)(2,1)S(1)} %all-to-all-done.2.late.rest_1_), channel_id=1, source_target_pairs={{0,8},{8,0},{16,24},{24,16},{1,9},{9,1},{17,25},{25,17},{2,10},{10... | collective-permute-start | bytes 1966088 | tf_op jit(solution)/shard_map/ppermute | solution.py:426
  80.0 16.0 %all-to-all-start.1 = ((bf16[8,3,16,512]{3,2,1,0:T(8,128)(2,1)}), bf16[8,3,16,512]{3,2,1,0:T(8,128)(2,1)S(1)}, u32[]{:S(2)}, u32[]{:S(2)}) async-start(bf16[8,3,16,512]{3,2,1,0:T(8,128)(2,1)} %get-tuple-element.29), calls=%async_computation.1 | async-start | bytes 786432 | tf_op jit(solution)/shard_map/all_to_all | solution.py:463
  83.7 19.1 %collective-permute-start.6 = (bf16[8,5,16,512]{3,2,1,0:T(8,128)(2,1)S(1)}, bf16[8,5,16,512]{3,2,1,0:T(8,128)(2,1)S(1)}, u32[]{:S(2)}, u32[]{:S(2)}) collective-permute-start(bf16[8,5,16,512]{3,2,1,0:T(8,128)(2,1)S(1)} %all-to-all-done.2.late.rest_1_), channel_id=1, source_target_pairs={{0,16},{8,24},{16,0},{24,8},{1,17},{9,25},{17,1},{25,9},{2,18},{10... | collective-permute-start | bytes 1966088 | tf_op jit(solution)/shard_map/ppermute | solution.py:426
  94.0 1.5 %copy-start = (bf16[5,1024,256]{2,1,0:T(8,128)(2,1)}, bf16[5,1024,256]{2,1,0:T(8,128)(2,1)S(1)}, u32[]{:S(2)}) copy-start(bf16[5,1024,256]{2,1,0:T(8,128)(2,1)S(1)} %get-tuple-element.31.left.rest_4_) | copy-start | bytes 7864324
  96.0 15.0 %copy-start.1 = (bf16[5,1024,256]{2,1,0:T(8,128)(2,1)S(1)}, bf16[5,1024,256]{2,1,0:T(8,128)(2,1)}, u32[]{:S(2)}) copy-start(bf16[5,1024,256]{2,1,0:T(8,128)(2,1)} %copy-done) | copy-start | bytes 7864324
  97.5 13.5 %collective-permute-start.7 = (bf16[8,8,16,512]{3,2,1,0:T(8,128)(2,1)S(1)}, bf16[8,8,16,512]{3,2,1,0:T(8,128)(2,1)S(1)}, u32[]{:S(2)}, u32[]{:S(2)}) collective-permute-start(bf16[8,8,16,512]{3,2,1,0:T(8,128)(2,1)S(1)} %after.8.rest_0_), channel_id=1, source_target_pairs={{0,8},{8,0},{16,24},{24,16},{1,9},{9,1},{17,25},{25,17},{2,10},{10... | collective-permute-start | bytes 3145736 | tf_op jit(solution)/shard_map/ppermute | solution.py:426
  102.8 8.3 %collective-permute-start.8 = (bf16[8,5,16,512]{3,2,1,0:T(8,128)(2,1)S(1)}, bf16[8,5,16,512]{3,2,1,0:T(8,128)(2,1)S(1)}, u32[]{:S(2)}, u32[]{:S(2)}) collective-permute-start(bf16[8,5,16,512]{3,2,1,0:T(8,128)(2,1)S(1)} %collective-permute-done.6.rest_1_), channel_id=1, source_target_pairs={{0,8},{8,0},{16,24},{24,16},{1,9},{9,1},{17,25},{25,17},{2,10},{10... | collective-permute-start | bytes 1966088 | tf_op jit(solution)/shard_map/ppermute | solution.py:426
  102.8 3.3 %collective-permute-start.9 = (bf16[8,3,16,512]{3,2,1,0:T(8,128)(2,1)S(1)}, bf16[8,3,16,512]{3,2,1,0:T(8,128)(2,1)S(1)}, u32[]{:S(2)}, u32[]{:S(2)}) collective-permute-start(bf16[8,3,16,512]{3,2,1,0:T(8,128)(2,1)S(1)} %after.7.late.done.rest_1_), channel_id=1, source_target_pairs={{0,8},{8,0},{16,24},{24,16},{1,9},{9,1},{17,25},{25,17},{2,10},{10... | collective-permute-start | bytes 1179656 | tf_op jit(solution)/shard_map/ppermute | solution.py:426
  104.5 12.8 %collective-permute-start.5 = (bf16[8,3,16,512]{3,2,1,0:T(8,128)(2,1)S(1)}, bf16[8,3,16,512]{3,2,1,0:T(8,128)(2,1)S(1)}, u32[]{:S(2)}, u32[]{:S(2)}) collective-permute-start(bf16[8,3,16,512]{3,2,1,0:T(8,128)(2,1)S(1)} %after.7.late.done.rest_1_), channel_id=1, source_target_pairs={{0,16},{8,24},{16,0},{24,8},{1,17},{9,25},{17,1},{25,9},{2,18},{10... | collective-permute-start | bytes 1179656 | tf_op jit(solution)/shard_map/ppermute | solution.py:426
  117.4 1.8 %collective-permute-start.10 = (bf16[8,3,16,512]{3,2,1,0:T(8,128)(2,1)S(1)}, bf16[8,3,16,512]{3,2,1,0:T(8,128)(2,1)S(1)}, u32[]{:S(2)}, u32[]{:S(2)}) collective-permute-start(bf16[8,3,16,512]{3,2,1,0:T(8,128)(2,1)S(1)} %after.9.rest_1_), channel_id=1, source_target_pairs={{0,8},{8,0},{16,24},{24,16},{1,9},{9,1},{17,25},{25,17},{2,10},{10... | collective-permute-start | bytes 1179656 | tf_op jit(solution)/shard_map/ppermute | solution.py:426
where the time goes:
time: 124 us; the launch traced here: 123 us
  Pallas kernels  50.4 us (41%)
  waiting for transfers between devices  44.7 us (36%)
  starting transfers between devices  24.7 us (20%)
  local copies, waits for them, and re-layouts  3.39 us (3%)
    all_to_all x3, waiting for transfers between devices, exchanged(): return lax.all_to_all(chunk, 'tm', split_axis=0, concat_axis=0, tiled=True)  31.6 us
    pallas_call x4, Pallas kernels, cross_products(): pl.pallas_call(functools.partial(cross_kernel, 2.0 / depth, side), grid_s...  22.5 us
    pallas_call x2, Pallas kernels, own_spectra(): pl.pallas_call(functools.partial(spectra_kernel, span * half, span), out_...  16.4 us
    all_to_all x3, starting transfers between devices, exchanged(): return lax.all_to_all(chunk, 'tm', split_axis=0, concat_axis=0, tiled=True)  13.2 us
    ppermute x9, waiting for transfers between devices, swapped(): return lax.ppermute(shard, axis, [(i, i ^ bit) for i in range(devices)])  6.92 us
    ppermute x2, starting transfers between devices, from_behind(): return lax.ppermute(shard, axis, pairs)  6.16 us
    ppermute x2, waiting for transfers between devices, from_behind(): return lax.ppermute(shard, axis, pairs)  6.14 us
    ppermute x9, starting transfers between devices, swapped(): return lax.ppermute(shard, axis, [(i, i ^ bit) for i in range(devices)])  5.36 us
  transfers between devices with their start and end apart: 14, of which 7 were waited for; matrix products, arithmetic and copies ran while one was open for 0% of the time, Pallas kernels for 33%

commit v1 on v0

--- a/solution.py
+++ b/solution.py
@@ -307,7 +307,9 @@
         ],
         compiler_params=pltpu.CompilerParams(vmem_limit_bytes=50 * MIB),
         cost_estimate=pl.CostEstimate(
-            flops=2 * channels * LANES * 896 * windows, bytes_accessed=2 * channels * slab, transcendentals=0
+            flops=2 * channels * LANES * 896 * windows,
+            bytes_accessed=(32 if half else 4) * channels * slab,
+            transcendentals=0,
         ),
         name=f"own_spectra_{half}",
     )(offsets, valid, record, rim, transform, rise, fall, parts)
@@ -452,6 +454,22 @@
     )(shard, done)
 
 
+def untouched_kernel(shard, done, out):
+    pass
+
+
+def after_in_place(shard, done):
+    anywhere = pl.BlockSpec(memory_space=pl.ANY)
+    return pl.pallas_call(
+        untouched_kernel,
+        out_shape=jax.ShapeDtypeStruct(shard.shape, shard.dtype),
+        in_specs=[anywhere, pl.BlockSpec(memory_space=pltpu.VMEM)],
+        out_specs=anywhere,
+        input_output_aliases={0: 0},
+        name="after_in_place",
+    )(shard, done)
+
+
 def per_device(record, whitening, offsets, window_valid):
     devices = lax.axis_size("tm")
     blocks = lax.axis_size("chan")
@@ -473,7 +491,7 @@
     views = record, inbox, offsets, window_valid, transform, rise, fall
     (early,), _ = own_spectra(*views, done, devices, 0)
     late, done = own_spectra(*views, parts, devices, 1)
-    early = after(exchanged(after(early, parts)), done)
+    early = after(exchanged(early), done)
     result, begin, rest = None, 0, []
     near_early = None if stacked else fanned(early)
     far_early = None if stacked else swapped(early, "chan", top)
@@ -491,10 +509,10 @@
             rest.append((left, far, begin))
         begin += mine.shape[1]
     if not stacked:
-        far_early, ready = fanned(after(far_early, mine)), None
+        far_early = fanned(after_in_place(far_early, done))
         for left, far, begin in rest:
-            far = fanned(after(far, ready))
-            result, ready = cross_products(left, far_early, far, result, begin, bins, blocks, 1)
+            far = fanned(after(far, done))
+            result, done = cross_products(left, far_early, far, result, begin, bins, blocks, 1)
     return result
 
 

time: 124 us -> 155 us (1.25)
  waiting for transfers between devices: 44.7 us -> 58.4 us
  starting transfers between devices: 24.7 us -> 36.4 us
  local copies, waits for them, and re-layouts: 3.39 us -> 8.64 us
    ppermute x2, waiting for transfers between devices: 6.14 us -> 23.1 us  [from_behind(): return lax.ppermute(shard, axis, pairs)]
    all_to_all x3, waiting for transfers between devices: 31.6 us -> 15.8 us  [exchanged(): return lax.all_to_all(chunk, 'tm', split_axis=0, concat_axis=0, tiled=True)]
    ppermute x9, waiting for transfers between devices: 6.92 us -> 19.5 us  [swapped(): return lax.ppermute(shard, axis, [(i, i ^ bit) for i in range(devices)])]
    all_to_all x3, starting transfers between devices: 13.2 us -> 25.3 us  [exchanged(): return lax.all_to_all(chunk, 'tm', split_axis=0, concat_axis=0, tiled=True)]
    unnamed x12 -> x26, local copies, waits for them, and re-layouts: 3.39 us -> 8.64 us
  transfers between devices with their start and end apart: 14 -> 14, of which waited for: 7 -> 9; matrix products, arithmetic and copies ran while one was open for 0% -> 0% of each run, Pallas kernels for 33% -> 21%
where the time goes in v1:
time: 155 us
  waiting for transfers between devices  58.4 us (38%)
  Pallas kernels  51 us (33%)
  starting transfers between devices  36.4 us (23%)
  local copies, waits for them, and re-layouts  8.64 us (6%)
    all_to_all x3, starting transfers between devices, exchanged(): return lax.all_to_all(chunk, 'tm', split_axis=0, concat_axis=0, tiled=True)  25.3 us
    ppermute x2, waiting for transfers between devices, from_behind(): return lax.ppermute(shard, axis, pairs)  23.1 us
    pallas_call x4, Pallas kernels, cross_products(): pl.pallas_call(functools.partial(cross_kernel, 2.0 / depth, side), grid_s...  22.7 us
    ppermute x9, waiting for transfers between devices, swapped(): return lax.ppermute(shard, axis, [(i, i ^ bit) for i in range(devices)])  19.5 us
    pallas_call x2, Pallas kernels, own_spectra(): pl.pallas_call(functools.partial(spectra_kernel, span * half, span), out_...  17.4 us
    all_to_all x3, waiting for transfers between devices, exchanged(): return lax.all_to_all(chunk, 'tm', split_axis=0, concat_axis=0, tiled=True)  15.8 us
    unnamed x26, local copies, waits for them, and re-layouts  8.64 us
    ppermute x2, starting transfers between devices, from_behind(): return lax.ppermute(shard, axis, pairs)  6.15 us
  transfers between devices with their start and end apart: 14, of which 9 were waited for; matrix products, arithmetic and copies ran while one was open for 0% of the time, Pallas kernels for 21%

profile of v1, /device:TPU:0, one launch (start us, length us, event | category | flops | bytes accessed | tf_op | source)
XLA Modules:
  0.0 154.5 jit_solution(856278278397715106)
XLA Ops:
  0.0 1.7 %outbox.1 = bf16[512,128]{1,0:T(8,128)(2,1)} custom-call(s32[16]{0:T(128)} %offsets.5, s32[16]{0:T(128)} %valid.5, f32[512,8192]{1,0:T(8,128)} %record.7), custom_call_target="tpu_custom_call" | custom-call | tf_op jit(solution)/shard_map/outbox/pallas_call | solution.py:78
  1.7 4.9 %collective-permute-start = (bf16[512,128]{1,0:T(8,128)(2,1)}, bf16[512,128]{1,0:T(8,128)(2,1)S(1)}, u32[]{:S(2)}, u32[]{:S(2)}) collective-permute-start(bf16[512,128]{1,0:T(8,128)(2,1)} %outbox.1), channel_id=1, source_target_pairs={{0,1},{1,2},{2,3},{3,4},{4,5},{5,6},{6,7},{8,9},{9,10},{10,11},{11... | collective-permute-start | bytes 393224 | tf_op jit(solution)/shard_map/ppermute | solution.py:30
  9.6 3.3 %border_parts.1 = (bf16[64,8,512]{2,1,0:T(8,128)(2,1)S(1)}, f32[8,128]{1,0:T(8,128)S(1)}) custom-call(bf16[512,128]{1,0:T(8,128)(2,1)S(1)} %collective-permute-done.inbox.rim, f32[512,8192]{1,0:T(8,128)} %record.7, bf16[2048,128]{1,0:T(8,128)(2,1)S(1)} %get-tuple-element.23.blocks, f32[384,128]{1,0:T(8,128)S(1)} %get-tuple-element.24.rise, ...), custom_call_target="tpu_custom_call" | custom-call | flops 402653184 | bytes 3670016 | tf_op jit(solution)/shard_map/border_parts/pallas_call | solution.py:169
  12.9 9.0 %own_spectra_0.1 = (bf16[8,8,16,512]{3,2,1,0:T(8,128)(2,1)}, f32[8,128]{1,0:T(8,128)}) custom-call(s32[16]{0:T(128)S(1)} %copy-done.10, s32[16]{0:T(128)S(1)} %copy-done.11, f32[512,8192]{1,0:T(8,128)} %record.7, bf16[512,128]{1,0:T(8,128)(2,1)S(1)} %collective-permute-done.inbox.rim, bf16[2048,128]{1,0:T(8,128)(2,1)S(1)} %get-tuple-element.23.blocks, ...), custom_call_target="tpu_custom_call" | custom-call | flops 939524096 | bytes 16777216 | tf_op jit(solution)/shard_map/own_spectra_0/pallas_call | solution.py:296
  22.0 6.7 %all-to-all-start = ((bf16[8,8,16,512]{3,2,1,0:T(8,128)(2,1)}), bf16[8,8,16,512]{3,2,1,0:T(8,128)(2,1)S(1)}, u32[]{:S(2)}, u32[]{:S(2)}) async-start(bf16[8,8,16,512]{3,2,1,0:T(8,128)(2,1)} %get-tuple-element.27), calls=%async_computation | async-start | bytes 2097152 | tf_op jit(solution)/shard_map/all_to_all | solution.py:481
  28.7 1.3 collective-permute-start.1
  30.0 22.9 %collective-permute-done.1.parts = bf16[64,8,512]{2,1,0:T(8,128)(2,1)S(1)} collective-permute-done((bf16[64,8,512]{2,1,0:T(8,128)(2,1)S(1)}, bf16[64,8,512]{2,1,0:T(8,128)(2,1)S(1)}, u32[]{:S(2)}, u32[]{:S(2)}) %collective-permute-start.1) | collective-permute-done | bytes 524320 | tf_op jit(solution)/shard_map/ppermute | solution.py:30
  52.9 8.4 %own_spectra_1.1 = (bf16[8,5,16,512]{3,2,1,0:T(8,128)(2,1)}, bf16[8,3,16,512]{3,2,1,0:T(8,128)(2,1)}, f32[8,128]{1,0:T(8,128)S(1)}) custom-call(s32[16]{0:T(128)S(1)} %copy-done.10, s32[16]{0:T(128)S(1)} %copy-done.11, f32[512,8192]{1,0:T(8,128)} %record.7, bf16[512,128]{1,0:T(8,128)(2,1)S(1)} %collective-permute-done.inbox.rim, ...), custom_call_target="tpu_custom_call" | custom-call | flops 939524096 | bytes 134217728 | tf_op jit(solution)/shard_map/own_spectra_1/pallas_call | solution.py:296
  61.3 14.9 %all-to-all-start.2 = ((bf16[8,5,16,512]{3,2,1,0:T(8,128)(2,1)}), bf16[8,5,16,512]{3,2,1,0:T(8,128)(2,1)S(1)}, u32[]{:S(2)}, u32[]{:S(2)}) async-start(bf16[8,5,16,512]{3,2,1,0:T(8,128)(2,1)} %get-tuple-element.31), calls=%async_computation.2 | async-start | bytes 1310720 | tf_op jit(solution)/shard_map/all_to_all | solution.py:481
  76.3 15.3 %all-to-all-done.2.late.rest_1_ = bf16[8,5,16,512]{3,2,1,0:T(8,128)(2,1)S(1)} async-done(((bf16[8,5,16,512]{3,2,1,0:T(8,128)(2,1)}), bf16[8,5,16,512]{3,2,1,0:T(8,128)(2,1)S(1)}, u32[]{:S(2)}, u32[]{:S(2)}) %all-to-all-start.2) | async-done | bytes 655392 | tf_op jit(solution)/shard_map/all_to_all | solution.py:481
  91.7 3.7 %all-to-all-start.1 = ((bf16[8,3,16,512]{3,2,1,0:T(8,128)(2,1)}), bf16[8,3,16,512]{3,2,1,0:T(8,128)(2,1)S(1)}, u32[]{:S(2)}, u32[]{:S(2)}) async-start(bf16[8,3,16,512]{3,2,1,0:T(8,128)(2,1)} %get-tuple-element.30), calls=%async_computation.1 | async-start | bytes 786432 | tf_op jit(solution)/shard_map/all_to_all | solution.py:481
  95.4 1.5 %collective-permute-start.4 = (bf16[8,8,16,512]{3,2,1,0:T(8,128)(2,1)S(1)}, bf16[8,8,16,512]{3,2,1,0:T(8,128)(2,1)S(1)}, u32[]{:S(2)}, u32[]{:S(2)}) collective-permute-start(bf16[8,8,16,512]{3,2,1,0:T(8,128)(2,1)S(1)} %after.4.early.rest_0_), channel_id=1, source_target_pairs={{0,16},{8,24},{16,0},{24,8},{1,17},{9,25},{17,1},{25,9},{2,18},{10... | collective-permute-start | bytes 3145736 | tf_op jit(solution)/shard_map/ppermute | solution.py:428
  96.9 1.7 %left_sides.2 = (bf16[5,1024,256]{2,1,0:T(8,128)(2,1)S(1)}, f32[8,128]{1,0:T(8,128)}) custom-call(bf16[8,8,16,512]{3,2,1,0:T(8,128)(2,1)S(1)} %after.4.early.rest_0_, bf16[8,5,16,512]{3,2,1,0:T(8,128)(2,1)S(1)} %all-to-all-done.2.late.rest_1_, f32[8,128]{1,0:T(8,128)S(1)} %get-tuple-element.29.done), custom_call_target="tpu_custom_call" | custom-call | tf_op jit(solution)/shard_map/left_sides/pallas_call | solution.py:337
  98.6 7.2 %cross_products.4 = (bf16[8,2,512,2048]{3,2,1,0:T(8,128)(2,1)}, f32[8,128]{1,0:T(8,128)S(1)}) custom-call(s32[1]{0:T(128)} %bitcast.me, bf16[5,1024,256]{2,1,0:T(8,128)(2,1)S(1)} %get-tuple-element.32.left.rest_4_, bf16[8,8,16,512]{3,2,1,0:T(8,128)(2,1)S(1)} %after.4.early.rest_0_, bf16[8,5,16,512]{3,2,1,0:T(8,128)(2,1)S(1)} %all-to-all-done.2.late.rest_1_, ...), custom_call_target="tpu_custom_call" | custom-call | flops 2684354560 | bytes 10485760 | tf_op jit(solution)/shard_map/cross_products/pallas_call | solution.py:403
  105.8 1.5 copy-done.5
  107.8 1.6 %collective-permute-start.7 = (bf16[8,5,16,512]{3,2,1,0:T(8,128)(2,1)S(1)}, bf16[8,5,16,512]{3,2,1,0:T(8,128)(2,1)}, u32[]{:S(2)}, u32[]{:S(2)}) collective-permute-start(bf16[8,5,16,512]{3,2,1,0:T(8,128)(2,1)S(1)} %all-to-all-done.2.late.rest_1_), channel_id=1, source_target_pairs={{0,16},{8,24},{16,0},{24,8},{1,17},{9,25},{17,1},{25,9},{2,18},{10... | collective-permute-start | bytes 1966088 | tf_op jit(solution)/shard_map/ppermute | solution.py:428
  110.6 5.2 %cross_products.5 = (bf16[8,2,512,2048]{3,2,1,0:T(8,128)(2,1)}, f32[8,128]{1,0:T(8,128)S(1)}) custom-call(s32[1]{0:T(128)} %bitcast.me, bf16[3,1024,256]{2,1,0:T(8,128)(2,1)S(1)} %get-tuple-element.34.left, bf16[8,8,16,512]{3,2,1,0:T(8,128)(2,1)S(1)} %after.4.early.rest_0_, ...), custom_call_target="tpu_custom_call", output_to_operand_aliasing={{0}: (6, {})} | custom-call | flops 1610612736 | bytes 6291456 | tf_op jit(solution)/shard_map/cross_products/pallas_call | solution.py:403
  116.4 5.0 %collective-permute-done.4.shard = bf16[8,8,16,512]{3,2,1,0:T(8,128)(2,1)S(1)} collective-permute-done((bf16[8,8,16,512]{3,2,1,0:T(8,128)(2,1)S(1)}, bf16[8,8,16,512]{3,2,1,0:T(8,128)(2,1)S(1)}, u32[]{:S(2)}, u32[]{:S(2)}) %collective-permute-start.4) | collective-permute-done | bytes 1048608 | tf_op jit(solution)/shard_map/ppermute | solution.py:428
  123.1 12.0 %collective-permute-done.7.shard = bf16[8,5,16,512]{3,2,1,0:T(8,128)(2,1)} collective-permute-done((bf16[8,5,16,512]{3,2,1,0:T(8,128)(2,1)S(1)}, bf16[8,5,16,512]{3,2,1,0:T(8,128)(2,1)}, u32[]{:S(2)}, u32[]{:S(2)}) %collective-permute-start.7) | collective-permute-done | bytes 655392 | tf_op jit(solution)/shard_map/ppermute | solution.py:428
  137.0 1.6 %collective-permute-start.6 = (bf16[8,3,16,512]{3,2,1,0:T(8,128)(2,1)S(1)}, bf16[8,3,16,512]{3,2,1,0:T(8,128)(2,1)S(1)}, u32[]{:S(2)}, u32[]{:S(2)}) collective-permute-start(bf16[8,3,16,512]{3,2,1,0:T(8,128)(2,1)S(1)} %after.5.late.rest_1_), channel_id=1, source_target_pairs={{0,16},{8,24},{16,0},{24,8},{1,17},{9,25},{17,1},{25,9},{2,18},{10... | collective-permute-start | bytes 1179656 | tf_op jit(solution)/shard_map/ppermute | solution.py:428
  140.3 1.7 %copy-done.6 = bf16[5,1024,256]{2,1,0:T(8,128)(2,1)S(1)} copy-done((bf16[5,1024,256]{2,1,0:T(8,128)(2,1)S(1)}, bf16[5,1024,256]{2,1,0:T(8,128)(2,1)}, u32[]{:S(2)}) %copy-start.6) | copy-done | bytes 2621464
  142.1 6.2 %cross_products.6 = (bf16[8,2,512,2048]{3,2,1,0:T(8,128)(2,1)}, f32[8,128]{1,0:T(8,128)S(1)}) custom-call(s32[1]{0:T(128)} %bitcast.me, bf16[5,1024,256]{2,1,0:T(8,128)(2,1)S(1)} %copy-done.6, bf16[8,8,16,512]{3,2,1,0:T(8,128)(2,1)S(1)} %copy-done.1, bf16[8,5,16,512]{3,2,1,0:T(8,128)(2,1)S(1)} %after.6.rest_1_, ...), custom_call_target="tpu_custom_call", output_to_operand_aliasing={{0}: (6, {})} | custom-call | flops 2684354560 | bytes 10485760 | tf_op jit(solution)/shard_map/cross_products/pallas_call | solution.py:403
  148.7 1.7 %collective-permute-done.10.rest_3_ = bf16[8,3,16,512]{3,2,1,0:T(8,128)(2,1)S(1)} collective-permute-done((bf16[8,3,16,512]{3,2,1,0:T(8,128)(2,1)S(1)}, bf16[8,3,16,512]{3,2,1,0:T(8,128)(2,1)S(1)}, u32[]{:S(2)}, u32[]{:S(2)}) %collective-permute-start.10) | collective-permute-done | bytes 393248 | tf_op jit(solution)/shard_map/ppermute | solution.py:428
  150.4 4.2 %cross_products.7 = (bf16[8,2,512,2048]{3,2,1,0:T(8,128)(2,1)}, f32[8,128]{1,0:T(8,128)}) custom-call(s32[1]{0:T(128)} %bitcast.me, bf16[3,1024,256]{2,1,0:T(8,128)(2,1)S(1)} %copy-done.4, bf16[8,8,16,512]{3,2,1,0:T(8,128)(2,1)S(1)} %copy-done.2, bf16[8,3,16,512]{3,2,1,0:T(8,128)(2,1)S(1)} %after.7.rest_1_, ...), custom_call_target="tpu_custom_call", output_to_operand_aliasing={{0}: (6, {})} | custom-call | flops 1610612736 | bytes 6291456 | tf_op jit(solution)/shard_map/cross_products/pallas_call | solution.py:403
  (46 shorter events, 11.2 us)
Async XLA Ops:
  0.0 12.9 %copy-start.10 = (s32[16]{0:T(128)S(1)}, s32[16]{0:T(128)}, u32[]{:S(2)}) copy-start(s32[16]{0:T(128)} %offsets.5) | copy-start | bytes 196
  0.0 12.9 %copy-start.11 = (s32[16]{0:T(128)S(1)}, s32[16]{0:T(128)}, u32[]{:S(2)}) copy-start(s32[16]{0:T(128)} %valid.5) | copy-start | bytes 196
  1.7 7.9 %collective-permute-start = (bf16[512,128]{1,0:T(8,128)(2,1)}, bf16[512,128]{1,0:T(8,128)(2,1)S(1)}, u32[]{:S(2)}, u32[]{:S(2)}) collective-permute-start(bf16[512,128]{1,0:T(8,128)(2,1)} %outbox.1), channel_id=1, source_target_pairs={{0,1},{1,2},{2,3},{3,4},{4,5},{5,6},{6,7},{8,9},{9,10},{10,11},{11... | collective-permute-start | bytes 393224 | tf_op jit(solution)/shard_map/ppermute | solution.py:30
  6.5 1.2 copy-start.7
  22.0 39.3 %all-to-all-start = ((bf16[8,8,16,512]{3,2,1,0:T(8,128)(2,1)}), bf16[8,8,16,512]{3,2,1,0:T(8,128)(2,1)S(1)}, u32[]{:S(2)}, u32[]{:S(2)}) async-start(bf16[8,8,16,512]{3,2,1,0:T(8,128)(2,1)} %get-tuple-element.27), calls=%async_computation | async-start | bytes 2097152 | tf_op jit(solution)/shard_map/all_to_all | solution.py:481
  28.7 24.2 %collective-permute-start.1 = (bf16[64,8,512]{2,1,0:T(8,128)(2,1)S(1)}, bf16[64,8,512]{2,1,0:T(8,128)(2,1)S(1)}, u32[]{:S(2)}, u32[]{:S(2)}) collective-permute-start(bf16[64,8,512]{2,1,0:T(8,128)(2,1)S(1)} %get-tuple-element.28), channel_id=1, source_target_pairs={{1,0},{2,1},{3,2},{4,3},{5,4},{6,5},{7,6},{9,8},{10,9},{11,10},{12... | collective-permute-start | bytes 1572872 | tf_op jit(solution)/shard_map/ppermute | solution.py:30
  61.3 30.4 %all-to-all-start.2 = ((bf16[8,5,16,512]{3,2,1,0:T(8,128)(2,1)}), bf16[8,5,16,512]{3,2,1,0:T(8,128)(2,1)S(1)}, u32[]{:S(2)}, u32[]{:S(2)}) async-start(bf16[8,5,16,512]{3,2,1,0:T(8,128)(2,1)} %get-tuple-element.31), calls=%async_computation.2 | async-start | bytes 1310720 | tf_op jit(solution)/shard_map/all_to_all | solution.py:481
  76.3 22.4 %collective-permute-start.2 = (bf16[8,8,16,512]{3,2,1,0:T(8,128)(2,1)S(1)}, bf16[8,8,16,512]{3,2,1,0:T(8,128)(2,1)}, u32[]{:S(2)}, u32[]{:S(2)}) collective-permute-start(bf16[8,8,16,512]{3,2,1,0:T(8,128)(2,1)S(1)} %after.4.early.rest_0_), channel_id=1, source_target_pairs={{0,8},{8,0},{16,24},{24,16},{1,9},{9,1},{17,25},{25,17},{2,10},{10... | collective-permute-start | bytes 3145736 | tf_op jit(solution)/shard_map/ppermute | solution.py:428
  91.7 6.9 %collective-permute-start.3 = (bf16[8,5,16,512]{3,2,1,0:T(8,128)(2,1)S(1)}, bf16[8,5,16,512]{3,2,1,0:T(8,128)(2,1)}, u32[]{:S(2)}, u32[]{:S(2)}) collective-permute-start(bf16[8,5,16,512]{3,2,1,0:T(8,128)(2,1)S(1)} %all-to-all-done.2.late.rest_1_), channel_id=1, source_target_pairs={{0,8},{8,0},{16,24},{24,16},{1,9},{9,1},{17,25},{25,17},{2,10},{10... | collective-permute-start | bytes 1966088 | tf_op jit(solution)/shard_map/ppermute | solution.py:428
  91.7 16.0 %all-to-all-start.1 = ((bf16[8,3,16,512]{3,2,1,0:T(8,128)(2,1)}), bf16[8,3,16,512]{3,2,1,0:T(8,128)(2,1)S(1)}, u32[]{:S(2)}, u32[]{:S(2)}) async-start(bf16[8,3,16,512]{3,2,1,0:T(8,128)(2,1)} %get-tuple-element.30), calls=%async_computation.1 | async-start | bytes 786432 | tf_op jit(solution)/shard_map/all_to_all | solution.py:481
  95.4 26.0 %collective-permute-start.4 = (bf16[8,8,16,512]{3,2,1,0:T(8,128)(2,1)S(1)}, bf16[8,8,16,512]{3,2,1,0:T(8,128)(2,1)S(1)}, u32[]{:S(2)}, u32[]{:S(2)}) collective-permute-start(bf16[8,8,16,512]{3,2,1,0:T(8,128)(2,1)S(1)} %after.4.early.rest_0_), channel_id=1, source_target_pairs={{0,16},{8,24},{16,0},{24,8},{1,17},{9,25},{17,1},{25,9},{2,18},{10... | collective-permute-start | bytes 3145736 | tf_op jit(solution)/shard_map/ppermute | solution.py:428
  105.8 1.5 copy-start.5
  107.8 2.9 %collective-permute-start.5 = (bf16[8,3,16,512]{3,2,1,0:T(8,128)(2,1)S(1)}, bf16[8,3,16,512]{3,2,1,0:T(8,128)(2,1)S(1)}, u32[]{:S(2)}, u32[]{:S(2)}) collective-permute-start(bf16[8,3,16,512]{3,2,1,0:T(8,128)(2,1)S(1)} %after.5.late.rest_1_), channel_id=1, source_target_pairs={{0,8},{8,0},{16,24},{24,16},{1,9},{9,1},{17,25},{25,17},{2,10},{10... | collective-permute-start | bytes 1179656 | tf_op jit(solution)/shard_map/ppermute | solution.py:428
  107.8 27.3 %collective-permute-start.7 = (bf16[8,5,16,512]{3,2,1,0:T(8,128)(2,1)S(1)}, bf16[8,5,16,512]{3,2,1,0:T(8,128)(2,1)}, u32[]{:S(2)}, u32[]{:S(2)}) collective-permute-start(bf16[8,5,16,512]{3,2,1,0:T(8,128)(2,1)S(1)} %all-to-all-done.2.late.rest_1_), channel_id=1, source_target_pairs={{0,16},{8,24},{16,0},{24,8},{1,17},{9,25},{17,1},{25,9},{2,18},{10... | collective-permute-start | bytes 1966088 | tf_op jit(solution)/shard_map/ppermute | solution.py:428
  110.6 10.8 %copy-start.3 = (bf16[3,1024,256]{2,1,0:T(8,128)(2,1)}, bf16[3,1024,256]{2,1,0:T(8,128)(2,1)S(1)}, u32[]{:S(2)}) copy-start(bf16[3,1024,256]{2,1,0:T(8,128)(2,1)S(1)} %get-tuple-element.34.left) | copy-start | bytes 4718596
  121.4 1.0 copy-start
  123.1 27.3 %copy-start.2 = (bf16[8,8,16,512]{3,2,1,0:T(8,128)(2,1)S(1)}, bf16[8,8,16,512]{3,2,1,0:T(8,128)(2,1)}, u32[]{:S(2)}) copy-start(bf16[8,8,16,512]{3,2,1,0:T(8,128)(2,1)} %after_in_place.1.rest_0_) | copy-start | bytes 3145732
  123.1 16.0 %collective-permute-start.8 = (bf16[8,8,16,512]{3,2,1,0:T(8,128)(2,1)}, bf16[8,8,16,512]{3,2,1,0:T(8,128)(2,1)S(1)}, u32[]{:S(2)}, u32[]{:S(2)}) collective-permute-start(bf16[8,8,16,512]{3,2,1,0:T(8,128)(2,1)} %after_in_place.1.rest_0_), channel_id=1, source_target_pairs={{0,8},{8,0},{16,24},{24,16},{1,9},{9,1},{17,25},{25,17},{2,10},{10... | collective-permute-start | bytes 3145736 | tf_op jit(solution)/shard_map/ppermute | solution.py:428
  136.9 2.2 %collective-permute-start.9 = (bf16[8,5,16,512]{3,2,1,0:T(8,128)(2,1)S(1)}, bf16[8,5,16,512]{3,2,1,0:T(8,128)(2,1)S(1)}, u32[]{:S(2)}, u32[]{:S(2)}) collective-permute-start(bf16[8,5,16,512]{3,2,1,0:T(8,128)(2,1)S(1)} %after.6.rest_1_), channel_id=1, source_target_pairs={{0,8},{8,0},{16,24},{24,16},{1,9},{9,1},{17,25},{25,17},{2,10},{10... | collective-permute-start | bytes 1966088 | tf_op jit(solution)/shard_map/ppermute | solution.py:428
  137.0 11.5 %collective-permute-start.6 = (bf16[8,3,16,512]{3,2,1,0:T(8,128)(2,1)S(1)}, bf16[8,3,16,512]{3,2,1,0:T(8,128)(2,1)S(1)}, u32[]{:S(2)}, u32[]{:S(2)}) collective-permute-start(bf16[8,3,16,512]{3,2,1,0:T(8,128)(2,1)S(1)} %after.5.late.rest_1_), channel_id=1, source_target_pairs={{0,16},{8,24},{16,0},{24,8},{1,17},{9,25},{17,1},{25,9},{2,18},{10... | collective-permute-start | bytes 1179656 | tf_op jit(solution)/shard_map/ppermute | solution.py:428
  139.1 1.2 copy-start.1
  140.3 1.7 %copy-start.6 = (bf16[5,1024,256]{2,1,0:T(8,128)(2,1)S(1)}, bf16[5,1024,256]{2,1,0:T(8,128)(2,1)}, u32[]{:S(2)}) copy-start(bf16[5,1024,256]{2,1,0:T(8,128)(2,1)} %copy-done.5) | copy-start | bytes 7864324
  142.1 8.3 %copy-start.4 = (bf16[3,1024,256]{2,1,0:T(8,128)(2,1)S(1)}, bf16[3,1024,256]{2,1,0:T(8,128)(2,1)}, u32[]{:S(2)}) copy-start(bf16[3,1024,256]{2,1,0:T(8,128)(2,1)} %copy-done.3) | copy-start | bytes 4718596
  148.6 1.8 %collective-permute-start.10 = (bf16[8,3,16,512]{3,2,1,0:T(8,128)(2,1)S(1)}, bf16[8,3,16,512]{3,2,1,0:T(8,128)(2,1)S(1)}, u32[]{:S(2)}, u32[]{:S(2)}) collective-permute-start(bf16[8,3,16,512]{3,2,1,0:T(8,128)(2,1)S(1)} %after.7.rest_1_), channel_id=1, source_target_pairs={{0,8},{8,0},{16,24},{24,16},{1,9},{9,1},{17,25},{25,17},{2,10},{10... | collective-permute-start | bytes 1179656 | tf_op jit(solution)/shard_map/ppermute | solution.py:428
  (3 other events, 1.9 us)
